TPU v7x, 128 devices: a whole 4x4x4 slice. The times are simulated.
128 devices in a mesh: rows: 32 (over y, z, core), cols: 4 (over x).
Axes of the slice: x: 4, y: 4, z: 4, core: 2. Of those that a mesh axis runs over, the one named last changes fastest.
Arguments:
- points: float32 [16, 1048576], P(None, ('rows', 'cols')), may hold values from -2 to 2
- coeffs: float32 [32, 1048576], P(None, ('rows', 'cols')), may hold values from -6 to 6
- velocity: float32 [32, 1048576], P(None, ('rows', 'cols')), may hold values from -4 to 4
- targets: float32 [32, 1048576], P(None, ('rows', 'cols')), may hold values from -6 to 6
- batch_index: int32 [2, 2048], replicated, may hold values from 0 to 1048575, as said below
- test_points: float32 [16, 4096], P(None, 'cols'), may hold values from -2 to 2
Outputs:
- coeffs_out: float32 [32, 1048576], P(None, ('rows', 'cols'))
- velocity_out: float32 [32, 1048576], P(None, ('rows', 'cols'))
- samples: float32 [32, 4096], P(None, 'cols')
Inputs may be any that keep to these rules, and one draw needn't show every extreme that they name: `batch_index`: row numbers of training points, 2048 in each step; a row may repeat within a step, and rows of low-numbered devices are drawn far more often than others.
All inputs are finite; a program needn't handle non-finite values.
Results may differ from a plain program's by a relative error of at most 0.0042.
Values sent between devices are 32-bit elements; how exact they have to be, the bound alone decides.
No kernel may reach another device: no remote copies, remote signals or barrier semaphores. Data moves between devices by JAX's collectives and lax.ppermute only.
A program may use at most 128 MiB of HBM per device.

v0:
```python
import math
import jax
import jax.numpy as jnp
from jax import lax
from jax.sharding import PartitionSpec as P

SCALE = 3.0**0.5 / 1.25


def matern_tile(points_block, queries):
    cross_term = jnp.dot(
        points_block.T, queries, precision=lax.Precision.HIGHEST, preferred_element_type=jnp.float32
    )
    sq_points = jnp.sum(points_block * points_block, axis=0)
    sq_queries = jnp.sum(queries * queries, axis=0)
    dist_sq = jnp.maximum(sq_points[:, None] + sq_queries[None, :] - 2.0 * cross_term, 0.0)
    scaled = SCALE * jnp.sqrt(dist_sq)
    return ((1.0 + scaled) * jnp.exp(-scaled)).astype(jnp.bfloat16)


def kernel_times(points, coeff_half, queries):
    query_count = queries.shape[1]
    blk_width = math.gcd(query_count, 512)
    blocks = queries.reshape(queries.shape[0], query_count // blk_width, blk_width).transpose(
        1, 0, 2
    )

    def apply_block(block):
        return jnp.dot(coeff_half, matern_tile(points, block), preferred_element_type=jnp.float32)

    results = lax.map(apply_block, blocks)
    return results.transpose(1, 0, 2).reshape(coeff_half.shape[0], query_count)


def per_device(points, coeffs, velocity, targets, batch_index, test_points):
    local_count = points.shape[1]
    row_start = lax.axis_index(("rows", "cols")) * local_count

    def take_owned(array, safe_rows, weights):
        return jnp.take(array, safe_rows, axis=1) * weights[None, :]

    steps_total = batch_index.shape[0]
    coeffs_now = coeffs
    velocity_now = velocity
    for step_no in range(steps_total):
        picked = batch_index[step_no]
        offset = picked - row_start
        inside = (offset >= 0) & (offset < local_count)
        owned_safe_rows = jnp.clip(offset, 0, local_count - 1)
        safe_rows = owned_safe_rows
        weights = inside.astype(jnp.float32)
        batch_points = lax.psum(take_owned(points, safe_rows, weights), ("rows", "cols"))
        partial_sums = kernel_times(points, coeffs_now.astype(jnp.bfloat16), batch_points)
        own_terms = take_owned(coeffs_now, safe_rows, weights) * 1.0 - take_owned(
            targets, safe_rows, weights
        )
        gradient = lax.psum(partial_sums + own_terms, ("rows", "cols"))
        summed = jnp.zeros_like(coeffs_now).at[:, safe_rows].add(gradient * weights[None, :])
        velocity_now = 0.9 * velocity_now - 0.5 * summed
        coeffs_now = coeffs_now + velocity_now
    coeff_half = coeffs_now.astype(jnp.bfloat16)
    partial_test = kernel_times(
        points, coeff_half, lax.all_gather(test_points, "cols", axis=1, tiled=True)
    )
    slab_sum = lax.psum_scatter(partial_test, "cols", scatter_dimension=1, tiled=True)
    slab_sum = lax.psum(slab_sum, "rows")
    return (coeffs_now, velocity_now, slab_sum)


def solution(mesh):
    return jax.shard_map(
        per_device,
        mesh=mesh,
        in_specs=(
            P(None, ("rows", "cols")),
            P(None, ("rows", "cols")),
            P(None, ("rows", "cols")),
            P(None, ("rows", "cols")),
            P(),
            P(None, "cols"),
        ),
        out_specs=(P(None, ("rows", "cols")), P(None, ("rows", "cols")), P(None, "cols")),
        check_vma=False,
    )
```

profile of v0, /device:TPU:1, one launch (start us, length us, event | category | flops | bytes accessed | tf_op | source)
XLA Modules:
  0.0 1088.0 jit_solution(15402246799207417307)
XLA Ops:
  9.6 3.5 copy.26
  13.1 9.8 gather_fusion
  25.7 9.8 gather_fusion.3
  40.1 3.6 copy.30
  43.7 9.8 gather_fusion.2
  53.6 9.8 gather_fusion.1
  64.4 104.7 %all-reduce.6.cloned.1.call-done = f32[4,16,512]{2,1,0:T(8,128)} async-done(((f32[4,16,512]{2,1,0:T(8,128)}), f32[4,16,512]{2,1,0:T(8,128)}) %all-reduce.6.cloned.1.call-update) | async-done | bytes 131088 | tf_op jit(solution)/shard_map/psum | solution.py:52
  169.1 109.0 %while.36 = (s32[]{:T(128)}, f32[4,32,512]{2,1,0:T(8,128)S(1)}, f32[8192]{0:T(1024)S(1)}, f32[4,16,512]{2,1,0:T(8,128)}, f32[16,8192]{1,0:T(8,128)S(1)}, /*index=5*/bf16[32,8192]{1,0:T(8,128)(2,1)S(1)}, s32[]{:T(128)}) while((s32[]{:T(128)}, f32[4,32,512]{2,1,0:T(8,128)S(1)}, f32[8192]{0:T(1024)S(1)}, f32[4,16,512]{2,1,0:T(8,128)}, ...), condition=%wide.region_4.6_spmd, body=%wide.region_2.5_spmd.sunk | while | flops 1111506432 | bytes 17993824 | solution.py:31
  170.0 23.8 %multiply_convert_fusion.6 = bf16[8192,512]{0,1:T(8,128)(2,1)S(1)} fusion(f32[16,8192]{1,0:T(8,128)S(1)} %get-tuple-element.416, f32[512]{0:T(512)S(1)} %fusion.69, f32[8192]{0:T(1024)S(1)} %get-tuple-element.414, f32[4,16,512]{2,1,0:T(8,128)} %get-tuple-element.415, s32[]{:T(128)S(6)} %copy.59), kind=kOutput, calls=%fused_computation.12.clone.1 | convolution fusion | flops 843055104 | bytes 8980484 | tf_op jit(solution)/shard_map/while/body/eval_jaxpr/dot_general | solution.py:11
  197.2 23.8 %multiply_convert_fusion.6 = bf16[8192,512]{0,1:T(8,128)(2,1)S(1)} fusion(f32[16,8192]{1,0:T(8,128)S(1)} %get-tuple-element.416, f32[512]{0:T(512)S(1)} %fusion.69, f32[8192]{0:T(1024)S(1)} %get-tuple-element.414, f32[4,16,512]{2,1,0:T(8,128)} %get-tuple-element.415, s32[]{:T(128)S(6)} %copy.59), kind=kOutput, calls=%fused_computation.12.clone.1 | convolution fusion | flops 843055104 | bytes 8980484 | tf_op jit(solution)/shard_map/while/body/eval_jaxpr/dot_general | solution.py:11
  224.4 23.8 %multiply_convert_fusion.6 = bf16[8192,512]{0,1:T(8,128)(2,1)S(1)} fusion(f32[16,8192]{1,0:T(8,128)S(1)} %get-tuple-element.416, f32[512]{0:T(512)S(1)} %fusion.69, f32[8192]{0:T(1024)S(1)} %get-tuple-element.414, f32[4,16,512]{2,1,0:T(8,128)} %get-tuple-element.415, s32[]{:T(128)S(6)} %copy.59), kind=kOutput, calls=%fused_computation.12.clone.1 | convolution fusion | flops 843055104 | bytes 8980484 | tf_op jit(solution)/shard_map/while/body/eval_jaxpr/dot_general | solution.py:11
  251.6 23.8 %multiply_convert_fusion.6 = bf16[8192,512]{0,1:T(8,128)(2,1)S(1)} fusion(f32[16,8192]{1,0:T(8,128)S(1)} %get-tuple-element.416, f32[512]{0:T(512)S(1)} %fusion.69, f32[8192]{0:T(1024)S(1)} %get-tuple-element.414, f32[4,16,512]{2,1,0:T(8,128)} %get-tuple-element.415, s32[]{:T(128)S(6)} %copy.59), kind=kOutput, calls=%fused_computation.12.clone.1 | convolution fusion | flops 843055104 | bytes 8980484 | tf_op jit(solution)/shard_map/while/body/eval_jaxpr/dot_general | solution.py:11
  281.3 9.8 gather_fusion.5
  291.1 3.6 copy.25
  294.7 131.7 %all-reduce.12.cloned.1.call-done = (f32[32,2048]{0,1:T(8,128)}, f32[4,16,512]{2,1,0:T(8,128)}) async-done(((f32[32,2048]{0,1:T(8,128)}, f32[4,16,512]{2,1,0:T(8,128)}), (f32[32,2048]{0,1:T(8,128)}, f32[4,16,512]{2,1,0:T(8,128)})) %all-reduce.12.cloned.1.call-update) | async-done | bytes 393232 | tf_op jit(solution)/shard_map/psum | solution.py:57
  426.4 15.7 %scatter_custom_fusion = f32[32,8192]{0,1:T(8,128)} fusion(s32[2048]{0:T(1024)S(1)} %bitcast.194, f32[]{:T(128)} %constant.138.clone.1, f32[32,2048]{0,1:T(8,128)} %get-tuple-element.272, f32[2048]{0:T(1024)S(1)} %bitcast.188), kind=kCustom, calls=%fused_computation.46 | custom fusion | flops 131072 | bytes 1318916 | tf_op jit(solution)/shard_map/scatter-add | solution.py:58
  442.1 7.4 fusion.38
  450.4 102.8 %while.37 = (s32[]{:T(128)}, f32[4,32,512]{2,1,0:T(8,128)S(1)}, f32[8192]{0:T(1024)S(1)}, f32[4,16,512]{2,1,0:T(8,128)S(1)}, f32[16,8192]{1,0:T(8,128)S(1)}, /*index=5*/bf16[32,8192]{1,0:T(8,128)(2,1)S(1)}, s32[]{:T(128)}) while((s32[]{:T(128)}, f32[4,32,512]{2,1,0:T(8,128)S(1)}, f32[8192]{0:T(1024)S(1)}, f32[4,16,512]{2,1,0:T(8,128)S(1)}, ...), condition=%wide.region_10.13_spmd, body=%wide.region_8.12_spmd.sunk | while | flops 1111506432 | bytes 17993824 | solution.py:31
  450.4 23.0 %multiply_convert_fusion.7 = bf16[8192,512]{0,1:T(8,128)(2,1)S(1)} fusion(f32[16,8192]{1,0:T(8,128)S(1)} %get-tuple-element.437, f32[512]{0:T(512)S(1)} %fusion.75, f32[8192]{0:T(1024)S(1)} %get-tuple-element.435, f32[4,16,512]{2,1,0:T(8,128)S(1)} %get-tuple-element.436, s32[]{:T(128)S(6)} %copy.67), kind=kOutput, calls=%fused_computation.24.clone.1 | convolution fusion | flops 843055104 | bytes 8980484 | tf_op jit(solution)/shard_map/while/body/eval_jaxpr/dot_general | solution.py:11
  476.1 23.1 %multiply_convert_fusion.7 = bf16[8192,512]{0,1:T(8,128)(2,1)S(1)} fusion(f32[16,8192]{1,0:T(8,128)S(1)} %get-tuple-element.437, f32[512]{0:T(512)S(1)} %fusion.75, f32[8192]{0:T(1024)S(1)} %get-tuple-element.435, f32[4,16,512]{2,1,0:T(8,128)S(1)} %get-tuple-element.436, s32[]{:T(128)S(6)} %copy.67), kind=kOutput, calls=%fused_computation.24.clone.1 | convolution fusion | flops 843055104 | bytes 8980484 | tf_op jit(solution)/shard_map/while/body/eval_jaxpr/dot_general | solution.py:11
  501.8 23.1 %multiply_convert_fusion.7 = bf16[8192,512]{0,1:T(8,128)(2,1)S(1)} fusion(f32[16,8192]{1,0:T(8,128)S(1)} %get-tuple-element.437, f32[512]{0:T(512)S(1)} %fusion.75, f32[8192]{0:T(1024)S(1)} %get-tuple-element.435, f32[4,16,512]{2,1,0:T(8,128)S(1)} %get-tuple-element.436, s32[]{:T(128)S(6)} %copy.67), kind=kOutput, calls=%fused_computation.24.clone.1 | convolution fusion | flops 843055104 | bytes 8980484 | tf_op jit(solution)/shard_map/while/body/eval_jaxpr/dot_general | solution.py:11
  527.5 23.1 %multiply_convert_fusion.7 = bf16[8192,512]{0,1:T(8,128)(2,1)S(1)} fusion(f32[16,8192]{1,0:T(8,128)S(1)} %get-tuple-element.437, f32[512]{0:T(512)S(1)} %fusion.75, f32[8192]{0:T(1024)S(1)} %get-tuple-element.435, f32[4,16,512]{2,1,0:T(8,128)S(1)} %get-tuple-element.436, s32[]{:T(128)S(6)} %copy.67), kind=kOutput, calls=%fused_computation.24.clone.1 | convolution fusion | flops 843055104 | bytes 8980484 | tf_op jit(solution)/shard_map/while/body/eval_jaxpr/dot_general | solution.py:11
  553.5 9.8 gather_fusion.4
  566.0 10.1 all_gather.3
  576.3 138.1 %all-reduce.8.cloned.1.call-done = f32[32,2048]{0,1:T(8,128)} async-done(((f32[32,2048]{0,1:T(8,128)}), f32[32,2048]{0,1:T(8,128)}) %all-reduce.8.cloned.1.call-update) | async-done | bytes 262160 | tf_op jit(solution)/shard_map/psum | solution.py:57
  714.3 15.7 %scatter_custom_fusion.1 = f32[32,8192]{0,1:T(8,128)} fusion(s32[2048]{0:T(1024)} %bitcast.193, f32[]{:T(128)} %constant.138.clone.1, f32[32,2048]{0,1:T(8,128)} %all-reduce.8.cloned.1.call-done, f32[2048]{0:T(1024)S(1)} %bitcast.185), kind=kCustom, calls=%fused_computation.44 | custom fusion | flops 131072 | bytes 2105856 | tf_op jit(solution)/shard_map/scatter-add | solution.py:58
  730.0 10.3 fusion.37
  741.1 210.8 %while.38 = (s32[]{:T(128)}, f32[8,32,512]{2,1,0:T(8,128)}, f32[8192]{0:T(1024)S(1)}, f32[8,16,512]{2,0,1:T(8,128)S(1)}, f32[16,8192]{1,0:T(8,128)S(1)}, /*index=5*/bf16[32,8192]{1,0:T(8,128)(2,1)S(1)}, s32[]{:T(128)}) while((s32[]{:T(128)}, f32[8,32,512]{2,1,0:T(8,128)}, f32[8192]{0:T(1024)S(1)}, f32[8,16,512]{2,0,1:T(8,128)S(1)}, ...), condition=%wide.region_15.18_spmd, body=%wide.region_13.17_spmd.sunk | while | flops 1111506432 | bytes 18059356 | solution.py:31
  741.2 23.0 %multiply_convert_fusion.8 = bf16[8192,512]{0,1:T(8,128)(2,1)S(1)} fusion(f32[16,8192]{1,0:T(8,128)S(1)} %get-tuple-element.458, f32[512]{0:T(512)S(1)} %multiply_reduce_fusion.3, f32[8192]{0:T(1024)S(1)} %get-tuple-element.456, f32[1,16,512]{2,0,1:T(1,128)S(1)} %constant_dynamic-slice_fusion.2), kind=kOutput, calls=%fused_computation.36.clone.1 | convolution fusion | flops 843055104 | bytes 8980480 | tf_op jit(solution)/shard_map/while/body/eval_jaxpr/dot_general | solution.py:11
  764.2 3.2 fusion.80
  767.5 23.0 %multiply_convert_fusion.8 = bf16[8192,512]{0,1:T(8,128)(2,1)S(1)} fusion(f32[16,8192]{1,0:T(8,128)S(1)} %get-tuple-element.458, f32[512]{0:T(512)S(1)} %multiply_reduce_fusion.3, f32[8192]{0:T(1024)S(1)} %get-tuple-element.456, f32[1,16,512]{2,0,1:T(1,128)S(1)} %constant_dynamic-slice_fusion.2), kind=kOutput, calls=%fused_computation.36.clone.1 | convolution fusion | flops 843055104 | bytes 8980480 | tf_op jit(solution)/shard_map/while/body/eval_jaxpr/dot_general | solution.py:11
  790.6 3.2 fusion.80
  793.9 23.0 %multiply_convert_fusion.8 = bf16[8192,512]{0,1:T(8,128)(2,1)S(1)} fusion(f32[16,8192]{1,0:T(8,128)S(1)} %get-tuple-element.458, f32[512]{0:T(512)S(1)} %multiply_reduce_fusion.3, f32[8192]{0:T(1024)S(1)} %get-tuple-element.456, f32[1,16,512]{2,0,1:T(1,128)S(1)} %constant_dynamic-slice_fusion.2), kind=kOutput, calls=%fused_computation.36.clone.1 | convolution fusion | flops 843055104 | bytes 8980480 | tf_op jit(solution)/shard_map/while/body/eval_jaxpr/dot_general | solution.py:11
  816.9 3.2 fusion.80
  820.2 23.0 %multiply_convert_fusion.8 = bf16[8192,512]{0,1:T(8,128)(2,1)S(1)} fusion(f32[16,8192]{1,0:T(8,128)S(1)} %get-tuple-element.458, f32[512]{0:T(512)S(1)} %multiply_reduce_fusion.3, f32[8192]{0:T(1024)S(1)} %get-tuple-element.456, f32[1,16,512]{2,0,1:T(1,128)S(1)} %constant_dynamic-slice_fusion.2), kind=kOutput, calls=%fused_computation.36.clone.1 | convolution fusion | flops 843055104 | bytes 8980480 | tf_op jit(solution)/shard_map/while/body/eval_jaxpr/dot_general | solution.py:11
  843.3 3.2 fusion.80
  846.6 23.0 %multiply_convert_fusion.8 = bf16[8192,512]{0,1:T(8,128)(2,1)S(1)} fusion(f32[16,8192]{1,0:T(8,128)S(1)} %get-tuple-element.458, f32[512]{0:T(512)S(1)} %multiply_reduce_fusion.3, f32[8192]{0:T(1024)S(1)} %get-tuple-element.456, f32[1,16,512]{2,0,1:T(1,128)S(1)} %constant_dynamic-slice_fusion.2), kind=kOutput, calls=%fused_computation.36.clone.1 | convolution fusion | flops 843055104 | bytes 8980480 | tf_op jit(solution)/shard_map/while/body/eval_jaxpr/dot_general | solution.py:11
  869.6 3.2 fusion.80
  872.9 23.0 %multiply_convert_fusion.8 = bf16[8192,512]{0,1:T(8,128)(2,1)S(1)} fusion(f32[16,8192]{1,0:T(8,128)S(1)} %get-tuple-element.458, f32[512]{0:T(512)S(1)} %multiply_reduce_fusion.3, f32[8192]{0:T(1024)S(1)} %get-tuple-element.456, f32[1,16,512]{2,0,1:T(1,128)S(1)} %constant_dynamic-slice_fusion.2), kind=kOutput, calls=%fused_computation.36.clone.1 | convolution fusion | flops 843055104 | bytes 8980480 | tf_op jit(solution)/shard_map/while/body/eval_jaxpr/dot_general | solution.py:11
  896.0 3.2 fusion.80
  899.3 23.0 %multiply_convert_fusion.8 = bf16[8192,512]{0,1:T(8,128)(2,1)S(1)} fusion(f32[16,8192]{1,0:T(8,128)S(1)} %get-tuple-element.458, f32[512]{0:T(512)S(1)} %multiply_reduce_fusion.3, f32[8192]{0:T(1024)S(1)} %get-tuple-element.456, f32[1,16,512]{2,0,1:T(1,128)S(1)} %constant_dynamic-slice_fusion.2), kind=kOutput, calls=%fused_computation.36.clone.1 | convolution fusion | flops 843055104 | bytes 8980480 | tf_op jit(solution)/shard_map/while/body/eval_jaxpr/dot_general | solution.py:11
  922.3 3.2 fusion.80
  925.6 23.0 %multiply_convert_fusion.8 = bf16[8192,512]{0,1:T(8,128)(2,1)S(1)} fusion(f32[16,8192]{1,0:T(8,128)S(1)} %get-tuple-element.458, f32[512]{0:T(512)S(1)} %multiply_reduce_fusion.3, f32[8192]{0:T(1024)S(1)} %get-tuple-element.456, f32[1,16,512]{2,0,1:T(1,128)S(1)} %constant_dynamic-slice_fusion.2), kind=kOutput, calls=%fused_computation.36.clone.1 | convolution fusion | flops 843055104 | bytes 8980480 | tf_op jit(solution)/shard_map/while/body/eval_jaxpr/dot_general | solution.py:11
  948.6 3.2 fusion.80
  953.8 21.0 %reduce-scatter.2.cloned.1.call-done = f32[32,1024]{1,0:T(8,128)} async-done(((f32[32,4096]{1,0:T(8,128)}), f32[32,1024]{1,0:T(8,128)}) %reduce-scatter.2.cloned.1.call-update) | async-done | bytes 131088 | tf_op jit(solution)/shard_map/reduce_scatter | solution.py:65
  974.8 3.6 copy.40
  978.4 3.6 copy.41
  982.0 97.5 %all-reduce.10.cloned.1.call-done = f32[32,1024]{1,0:T(8,128)} async-done(((f32[32,1024]{1,0:T(8,128)}), f32[32,1024]{1,0:T(8,128)}) %all-reduce.10.cloned.1.call-update) | async-done | bytes 131088 | tf_op jit(solution)/shard_map/psum | solution.py:66
  (87 shorter events, 46.6 us)
Async XLA Ops:
  7.2 30.1 %copy-start.1 = (f32[16,8192]{1,0:T(8,128)S(1)}, f32[16,8192]{1,0:T(8,128)}, u32[]{:S(2)}) copy-start(f32[16,8192]{1,0:T(8,128)} %param.16) | copy-start | bytes 1572868
  7.2 30.2 %copy-start = (f32[32,8192]{1,0:T(8,128)S(1)}, f32[32,8192]{1,0:T(8,128)}, u32[]{:S(2)}) copy-start(f32[32,8192]{1,0:T(8,128)} %param.17) | copy-start | bytes 3145732
  7.2 161.9 %all-reduce.6.cloned.1.call-start = ((), (), s32[]{:S(2)}) async-start(), calls=%async_computation.1 | async-start | bytes 262144 | tf_op jit(solution)/shard_map/psum | solution.py:52
  8.1 29.2 %copy-start.5 = (f32[1,2048]{1,0:T(1,128)}, f32[1,2048]{1,0:T(1,128)S(1)}, u32[]{:S(2)}) copy-start(f32[1,2048]{1,0:T(1,128)S(1)} %get-tuple-element.283) | copy-start | bytes 24580
  25.6 400.7 %all-reduce.12.cloned.1.call-start = ((), (), s32[]{:S(2)}) async-start(), calls=%async_computation.5 | async-start | bytes 2359296 | tf_op jit(solution)/shard_map/psum | solution.py:57
  25.7 27.9 %copy-start.8 = (pred[2048]{0:T(1024)(128)(4,1)}, pred[2048]{0:T(1024)(128)(4,1)S(1)}, u32[]{:S(2)}) copy-start(pred[2048]{0:T(1024)(128)(4,1)S(1)} %compare_and_fusion) | copy-start | bytes 6148
  169.1 109.3 %copy-start.3 = (f32[2048,32]{1,0:T(8,128)S(1)}, f32[2048,32]{1,0:T(8,128)}, u32[]{:S(2)}) copy-start(f32[2048,32]{1,0:T(8,128)} %gather_fusion.2) | copy-start | bytes 786436
  281.0 433.3 %all-reduce.8.cloned.1.call-start = ((), (), s32[]{:S(2)}) async-start(), calls=%async_computation.2 | async-start | bytes 2097152 | tf_op jit(solution)/shard_map/psum | solution.py:57
  442.1 8.3 copy-start.4
  450.4 113.0 %copy-start.2 = (f32[2048,32]{1,0:T(8,128)S(1)}, f32[2048,32]{1,0:T(8,128)}, u32[]{:S(2)}) copy-start(f32[2048,32]{1,0:T(8,128)} %gather_fusion.5) | copy-start | bytes 786436
  450.4 113.0 %copy-start.6 = (f32[1,2048]{1,0:T(1,128)S(1)}, f32[1,2048]{1,0:T(1,128)}, u32[]{:S(2)}) copy-start(f32[1,2048]{1,0:T(1,128)} %copy-done.5) | copy-start | bytes 24580
  450.4 113.0 %copy-start.9 = (pred[2048]{0:T(1024)(128)(4,1)S(1)}, pred[2048]{0:T(1024)(128)(4,1)}, u32[]{:S(2)}) copy-start(pred[2048]{0:T(1024)(128)(4,1)} %copy-done.8) | copy-start | bytes 6148
  553.2 12.9 %copy-start.7 = (f32[16,1024]{1,0:T(8,128)S(1)}, f32[16,1024]{1,0:T(8,128)}, u32[]{:S(2)}) copy-start(f32[16,1024]{1,0:T(8,128)} %param.21) | copy-start | bytes 196612
  566.0 408.8 %reduce-scatter.2.cloned.1.call-start = ((), (), s32[]{:S(2)}) async-start(), calls=%async_computation.3 | async-start | bytes 655360 | tf_op jit(solution)/shard_map/reduce_scatter | solution.py:65
  953.8 125.7 %all-reduce.10.cloned.1.call-start = ((), (), s32[]{:S(2)}) async-start(), calls=%async_computation.4 | async-start | bytes 262144 | tf_op jit(solution)/shard_map/psum | solution.py:66
Sparse Core Ops, SparseCore 0:
  25.7 143.2 all-reduce.5
  281.2 145.1 all-reduce.11
  566.1 148.1 all-reduce.7
  953.9 20.8 reduce-scatter.1
  978.2 101.2 all-reduce.9
where the time goes:
time: 1100 us; the launch traced here: 1090 us
  waiting for transfers between devices  493 us (45%)
  matrix products  419 us (38%)
  local copies, waits for them, and re-layouts  87.6 us (8%)
  other arithmetic  63.8 us (6%)
  between operations  14.4 us (1%)
    dot_general x16, matrix products, matern_tile(): jnp.dot(points_block.T, queries, precision=lax.Precision.HIGHEST, preferr...  372 us
    psum x2, waiting for transfers between devices, per_device(): gradient = lax.psum(partial_sums + own_terms, ('rows', 'cols'))  270 us
    psum x1, waiting for transfers between devices, per_device(): lax.psum(take_owned(points, safe_rows, weights), ('rows', 'cols'))  105 us
    psum x1, waiting for transfers between devices, per_device(): slab_sum = lax.psum(slab_sum, 'rows')  97.5 us
    gather x6, local copies, waits for them, and re-layouts, take_owned(): return jnp.take(array, safe_rows, axis=1) * weights[None, :]  58.9 us
    dot_general x16, matrix products, apply_block(): jnp.dot(coeff_half, matern_tile(points, block), preferred_element_type=jn...  46.8 us
    scatter-add x2, other arithmetic, per_device(): jnp.zeros_like(coeffs_now).at[:, safe_rows].add(gradient * weights[None, :])  31.4 us
    unnamed x28, local copies, waits for them, and re-layouts  22.4 us
  transfers between devices with their start and end apart: 5, of which 5 were waited for; matrix products, arithmetic and copies ran while one was open for 5% of the time, Pallas kernels for 0%

commit v1 on v0

--- a/solution.py
+++ b/solution.py
@@ -49,7 +49,9 @@
         owned_safe_rows = jnp.clip(offset, 0, local_count - 1)
         safe_rows = owned_safe_rows
         weights = inside.astype(jnp.float32)
-        batch_points = lax.psum(take_owned(points, safe_rows, weights), ("rows", "cols"))
+        own = take_owned(points, safe_rows, weights)
+        parts = lax.all_gather(own, ("rows", "cols"), axis=0, tiled=False)
+        batch_points = parts.sum(axis=0)
         partial_sums = kernel_times(points, coeffs_now.astype(jnp.bfloat16), batch_points)
         own_terms = take_owned(coeffs_now, safe_rows, weights) * 1.0 - take_owned(
             targets, safe_rows, weights

time: 1100 us -> 1040 us (0.945)
  waiting for transfers between devices: 493 us -> 423 us
  starting transfers between devices: 0.38 us -> 11.8 us
    psum x1 -> x0, waiting for transfers between devices: 105 us -> none  [per_device(): lax.psum(take_owned(points, safe_rows, weights), ('rows', 'cols'))]
    all_gather x0 -> x2, waiting for transfers between devices: none -> 51.3 us  [per_device(): parts = lax.all_gather(own, ('rows', 'cols'), axis=0, tiled=False)]
    psum x2, waiting for transfers between devices: 270 us -> 254 us  [per_device(): gradient = lax.psum(partial_sums + own_terms, ('rows', 'cols'))]
    reduce_sum x0 -> x2, other arithmetic: none -> 13.2 us  [per_device(): batch_points = parts.sum(axis=0)]
    psum x2, starting transfers between devices: 0.26 us -> 11.6 us  [per_device(): gradient = lax.psum(partial_sums + own_terms, ('rows', 'cols'))]
    gather x6 -> x8, local copies, waits for them, and re-layouts: 58.9 us -> 53 us  [take_owned(): return jnp.take(array, safe_rows, axis=1) * weights[None, :]]
    unnamed x28 -> x24, local copies, waits for them, and re-layouts: 22.4 us -> 22.4 us
  transfers between devices with their start and end apart: 5 -> 6, of which waited for: 5 -> 5; matrix products, arithmetic and copies ran while one was open for 5% -> 17% of each run, Pallas kernels for 0% -> 0%
where the time goes in v1:
time: 1040 us; the launch traced here: 1030 us
  waiting for transfers between devices  423 us (41%)
  matrix products  415 us (40%)
  local copies, waits for them, and re-layouts  80.3 us (8%)
  other arithmetic  71.8 us (7%)
  between operations  14.7 us (1%)
  starting transfers between devices  11.8 us (1%)
    dot_general x16, matrix products, matern_tile(): jnp.dot(points_block.T, queries, precision=lax.Precision.HIGHEST, preferr...  369 us
    psum x2, waiting for transfers between devices, per_device(): gradient = lax.psum(partial_sums + own_terms, ('rows', 'cols'))  254 us
    psum x1, waiting for transfers between devices, per_device(): slab_sum = lax.psum(slab_sum, 'rows')  97.2 us
    gather x8, local copies, waits for them, and re-layouts, take_owned(): return jnp.take(array, safe_rows, axis=1) * weights[None, :]  53 us
    all_gather x2, waiting for transfers between devices, per_device(): parts = lax.all_gather(own, ('rows', 'cols'), axis=0, tiled=False)  51.3 us
    dot_general x16, matrix products, apply_block(): jnp.dot(coeff_half, matern_tile(points, block), preferred_element_type=jn...  46.8 us
    scatter-add x2, other arithmetic, per_device(): jnp.zeros_like(coeffs_now).at[:, safe_rows].add(gradient * weights[None, :])  31.4 us
    unnamed x24, local copies, waits for them, and re-layouts  22.4 us
  transfers between devices with their start and end apart: 6, of which 5 were waited for; matrix products, arithmetic and copies ran while one was open for 17% of the time, Pallas kernels for 0%

profile of v1, /device:TPU:1, one launch (start us, length us, event | category | flops | bytes accessed | tf_op | source)
XLA Modules:
  0.0 1026.8 jit_solution(1262902991214102936)
XLA Ops:
  9.5 3.5 copy.62
  13.0 7.6 gather_fusion
  21.7 7.6 gather_fusion.3
  33.3 3.6 copy.67
  36.9 7.6 gather_fusion.2
  44.6 9.8 gather_fusion.1
  54.5 51.3 %all-gather.5.cloned.1.call-done = f32[2048,2048]{1,0:T(8,128)} async-done(((f32[16,2048]{1,0:T(8,128)}), f32[2048,2048]{1,0:T(8,128)}) %all-gather.5.cloned.1.call-update) | async-done | bytes 16777232 | tf_op jit(solution)/shard_map/all_gather | solution.py:53
  105.8 6.6 reduce_sum.75
  112.5 102.9 %while.36 = (s32[]{:T(128)}, f32[4,32,512]{2,1,0:T(8,128)S(1)}, f32[8192]{0:T(1024)S(1)}, f32[4,16,512]{2,0,1:T(4,128)S(1)}, f32[16,8192]{1,0:T(8,128)S(1)}, /*index=5*/bf16[32,8192]{1,0:T(8,128)(2,1)S(1)}, s32[]{:T(128)}) while((s32[]{:T(128)}, f32[4,32,512]{2,1,0:T(8,128)S(1)}, f32[8192]{0:T(1024)S(1)}, f32[4,16,512]{2,0,1:T(4,128)S(1)}, ...), condition=%wide.region_4.6_spmd, body=%wide.region_2.5_spmd.sunk | while | flops 1111506432 | bytes 18059356 | solution.py:31
  112.6 23.0 %multiply_convert_fusion.6 = bf16[8192,512]{0,1:T(8,128)(2,1)S(1)} fusion(f32[16,8192]{1,0:T(8,128)S(1)} %get-tuple-element.462, f32[512]{0:T(512)S(1)} %multiply_reduce_fusion.7, f32[8192]{0:T(1024)S(1)} %get-tuple-element.460, f32[1,16,512]{2,0,1:T(1,128)S(1)} %constant_dynamic-slice_fusion.6), kind=kOutput, calls=%fused_computation.12.clone.1 | convolution fusion | flops 843055104 | bytes 8980480 | tf_op jit(solution)/shard_map/while/body/eval_jaxpr/dot_general | solution.py:11
  138.3 23.0 %multiply_convert_fusion.6 = bf16[8192,512]{0,1:T(8,128)(2,1)S(1)} fusion(f32[16,8192]{1,0:T(8,128)S(1)} %get-tuple-element.462, f32[512]{0:T(512)S(1)} %multiply_reduce_fusion.7, f32[8192]{0:T(1024)S(1)} %get-tuple-element.460, f32[1,16,512]{2,0,1:T(1,128)S(1)} %constant_dynamic-slice_fusion.6), kind=kOutput, calls=%fused_computation.12.clone.1 | convolution fusion | flops 843055104 | bytes 8980480 | tf_op jit(solution)/shard_map/while/body/eval_jaxpr/dot_general | solution.py:11
  164.0 23.0 %multiply_convert_fusion.6 = bf16[8192,512]{0,1:T(8,128)(2,1)S(1)} fusion(f32[16,8192]{1,0:T(8,128)S(1)} %get-tuple-element.462, f32[512]{0:T(512)S(1)} %multiply_reduce_fusion.7, f32[8192]{0:T(1024)S(1)} %get-tuple-element.460, f32[1,16,512]{2,0,1:T(1,128)S(1)} %constant_dynamic-slice_fusion.6), kind=kOutput, calls=%fused_computation.12.clone.1 | convolution fusion | flops 843055104 | bytes 8980480 | tf_op jit(solution)/shard_map/while/body/eval_jaxpr/dot_general | solution.py:11
  189.7 23.0 %multiply_convert_fusion.6 = bf16[8192,512]{0,1:T(8,128)(2,1)S(1)} fusion(f32[16,8192]{1,0:T(8,128)S(1)} %get-tuple-element.462, f32[512]{0:T(512)S(1)} %multiply_reduce_fusion.7, f32[8192]{0:T(1024)S(1)} %get-tuple-element.460, f32[1,16,512]{2,0,1:T(1,128)S(1)} %constant_dynamic-slice_fusion.6), kind=kOutput, calls=%fused_computation.12.clone.1 | convolution fusion | flops 843055104 | bytes 8980480 | tf_op jit(solution)/shard_map/while/body/eval_jaxpr/dot_general | solution.py:11
  218.3 11.6 %all-reduce.6.cloned.1.call-start = ((), (), s32[]{:S(2)}) async-start(), calls=%async_computation.2 | async-start | bytes 2097152 | tf_op jit(solution)/shard_map/psum | solution.py:59
  229.9 9.8 gather_fusion.5
  239.7 3.6 copy.61
  243.3 6.7 reduce_sum.76
  250.1 114.9 %all-reduce.4.cloned.1.call-done = f32[32,2048]{0,1:T(8,128)} async-done(((f32[32,2048]{0,1:T(8,128)}), f32[32,2048]{0,1:T(8,128)}) %all-reduce.4.cloned.1.call-update) | async-done | bytes 262160 | tf_op jit(solution)/shard_map/psum | solution.py:59
  364.9 15.7 %scatter_custom_fusion = f32[32,8192]{0,1:T(8,128)} fusion(s32[2048]{0:T(1024)S(1)} %bitcast.192, f32[]{:T(128)} %constant.139.clone.1, f32[32,2048]{0,1:T(8,128)} %all-reduce.4.cloned.1.call-done, f32[2048]{0:T(1024)S(1)} %bitcast.186), kind=kCustom, calls=%fused_computation.42 | custom fusion | flops 131072 | bytes 1318916 | tf_op jit(solution)/shard_map/scatter-add | solution.py:60
  380.6 7.5 fusion.30
  389.0 102.9 %while.37 = (s32[]{:T(128)}, f32[4,32,512]{2,1,0:T(8,128)S(1)}, f32[8192]{0:T(1024)S(1)}, f32[4,16,512]{2,0,1:T(4,128)S(1)}, f32[16,8192]{1,0:T(8,128)S(1)}, /*index=5*/bf16[32,8192]{1,0:T(8,128)(2,1)S(1)}, s32[]{:T(128)}) while((s32[]{:T(128)}, f32[4,32,512]{2,1,0:T(8,128)S(1)}, f32[8192]{0:T(1024)S(1)}, f32[4,16,512]{2,0,1:T(4,128)S(1)}, ...), condition=%wide.region_10.13_spmd, body=%wide.region_8.12_spmd.sunk | while | flops 1111506432 | bytes 18059356 | solution.py:31
  389.1 23.0 %multiply_convert_fusion.7 = bf16[8192,512]{0,1:T(8,128)(2,1)S(1)} fusion(f32[16,8192]{1,0:T(8,128)S(1)} %get-tuple-element.483, f32[512]{0:T(512)S(1)} %multiply_reduce_fusion.8, f32[8192]{0:T(1024)S(1)} %get-tuple-element.481, f32[1,16,512]{2,0,1:T(1,128)S(1)} %constant_dynamic-slice_fusion.7), kind=kOutput, calls=%fused_computation.22.clone.1 | convolution fusion | flops 843055104 | bytes 8980480 | tf_op jit(solution)/shard_map/while/body/eval_jaxpr/dot_general | solution.py:11
  414.8 23.0 %multiply_convert_fusion.7 = bf16[8192,512]{0,1:T(8,128)(2,1)S(1)} fusion(f32[16,8192]{1,0:T(8,128)S(1)} %get-tuple-element.483, f32[512]{0:T(512)S(1)} %multiply_reduce_fusion.8, f32[8192]{0:T(1024)S(1)} %get-tuple-element.481, f32[1,16,512]{2,0,1:T(1,128)S(1)} %constant_dynamic-slice_fusion.7), kind=kOutput, calls=%fused_computation.22.clone.1 | convolution fusion | flops 843055104 | bytes 8980480 | tf_op jit(solution)/shard_map/while/body/eval_jaxpr/dot_general | solution.py:11
  440.5 23.0 %multiply_convert_fusion.7 = bf16[8192,512]{0,1:T(8,128)(2,1)S(1)} fusion(f32[16,8192]{1,0:T(8,128)S(1)} %get-tuple-element.483, f32[512]{0:T(512)S(1)} %multiply_reduce_fusion.8, f32[8192]{0:T(1024)S(1)} %get-tuple-element.481, f32[1,16,512]{2,0,1:T(1,128)S(1)} %constant_dynamic-slice_fusion.7), kind=kOutput, calls=%fused_computation.22.clone.1 | convolution fusion | flops 843055104 | bytes 8980480 | tf_op jit(solution)/shard_map/while/body/eval_jaxpr/dot_general | solution.py:11
  466.2 23.0 %multiply_convert_fusion.7 = bf16[8192,512]{0,1:T(8,128)(2,1)S(1)} fusion(f32[16,8192]{1,0:T(8,128)S(1)} %get-tuple-element.483, f32[512]{0:T(512)S(1)} %multiply_reduce_fusion.8, f32[8192]{0:T(1024)S(1)} %get-tuple-element.481, f32[1,16,512]{2,0,1:T(1,128)S(1)} %constant_dynamic-slice_fusion.7), kind=kOutput, calls=%fused_computation.22.clone.1 | convolution fusion | flops 843055104 | bytes 8980480 | tf_op jit(solution)/shard_map/while/body/eval_jaxpr/dot_general | solution.py:11
  492.2 9.8 gather_fusion.4
  504.7 9.6 all_gather.19
  514.4 138.7 %all-reduce.6.cloned.1.call-done = f32[32,2048]{0,1:T(8,128)} async-done(((f32[32,2048]{0,1:T(8,128)}), f32[32,2048]{0,1:T(8,128)}) %all-reduce.6.cloned.1.call-update) | async-done | bytes 262160 | tf_op jit(solution)/shard_map/psum | solution.py:59
  653.2 15.7 %scatter_custom_fusion.1 = f32[32,8192]{0,1:T(8,128)} fusion(s32[2048]{0:T(1024)} %bitcast.191, f32[]{:T(128)} %constant.139.clone.1, f32[32,2048]{0,1:T(8,128)} %all-reduce.6.cloned.1.call-done, f32[2048]{0:T(1024)S(1)} %bitcast.183), kind=kCustom, calls=%fused_computation.40 | custom fusion | flops 131072 | bytes 2105856 | tf_op jit(solution)/shard_map/scatter-add | solution.py:60
  668.8 10.3 %fusion.29 = (bf16[32,8192]{0,1:T(8,128)(2,1)S(1)}, f32[32,8192]{0,1:T(8,128)}, f32[32,8192]{0,1:T(8,128)}) fusion(f32[32,8192]{0,1:T(8,128)} %get-tuple-element.324, f32[32,8192]{0,1:T(8,128)} %scatter_custom_fusion.1, f32[32,8192]{0,1:T(8,128)} %scatter_custom_fusion, f32[32,8192]{0,1:T(8,128)} %copy.61), kind=kLoop, calls=%fused_computation.76 | loop fusion | flops 2097152 | bytes 6815744 | tf_op jit(solution)/shard_map/convert_element_type | solution.py:63
  680.0 210.8 %while.38 = (s32[]{:T(128)}, f32[8,32,512]{2,1,0:T(8,128)}, f32[8192]{0:T(1024)S(1)}, f32[8,16,512]{2,0,1:T(8,128)S(1)}, f32[16,8192]{1,0:T(8,128)S(1)}, /*index=5*/bf16[32,8192]{1,0:T(8,128)(2,1)S(1)}, s32[]{:T(128)}) while((s32[]{:T(128)}, f32[8,32,512]{2,1,0:T(8,128)}, f32[8192]{0:T(1024)S(1)}, f32[8,16,512]{2,0,1:T(8,128)S(1)}, ...), condition=%wide.region_15.18_spmd, body=%wide.region_13.17_spmd.sunk | while | flops 1111506432 | bytes 18059356 | solution.py:31
  680.0 23.0 %multiply_convert_fusion.8 = bf16[8192,512]{0,1:T(8,128)(2,1)S(1)} fusion(f32[16,8192]{1,0:T(8,128)S(1)} %get-tuple-element.504, f32[512]{0:T(512)S(1)} %multiply_reduce_fusion.9, f32[8192]{0:T(1024)S(1)} %get-tuple-element.502, f32[1,16,512]{2,0,1:T(1,128)S(1)} %constant_dynamic-slice_fusion.8), kind=kOutput, calls=%fused_computation.32.clone.1 | convolution fusion | flops 843055104 | bytes 8980480 | tf_op jit(solution)/shard_map/while/body/eval_jaxpr/dot_general | solution.py:11
  703.1 3.2 fusion.64
  706.4 23.0 %multiply_convert_fusion.8 = bf16[8192,512]{0,1:T(8,128)(2,1)S(1)} fusion(f32[16,8192]{1,0:T(8,128)S(1)} %get-tuple-element.504, f32[512]{0:T(512)S(1)} %multiply_reduce_fusion.9, f32[8192]{0:T(1024)S(1)} %get-tuple-element.502, f32[1,16,512]{2,0,1:T(1,128)S(1)} %constant_dynamic-slice_fusion.8), kind=kOutput, calls=%fused_computation.32.clone.1 | convolution fusion | flops 843055104 | bytes 8980480 | tf_op jit(solution)/shard_map/while/body/eval_jaxpr/dot_general | solution.py:11
  729.4 3.2 fusion.64
  732.7 23.0 %multiply_convert_fusion.8 = bf16[8192,512]{0,1:T(8,128)(2,1)S(1)} fusion(f32[16,8192]{1,0:T(8,128)S(1)} %get-tuple-element.504, f32[512]{0:T(512)S(1)} %multiply_reduce_fusion.9, f32[8192]{0:T(1024)S(1)} %get-tuple-element.502, f32[1,16,512]{2,0,1:T(1,128)S(1)} %constant_dynamic-slice_fusion.8), kind=kOutput, calls=%fused_computation.32.clone.1 | convolution fusion | flops 843055104 | bytes 8980480 | tf_op jit(solution)/shard_map/while/body/eval_jaxpr/dot_general | solution.py:11
  755.8 3.2 fusion.64
  759.1 23.0 %multiply_convert_fusion.8 = bf16[8192,512]{0,1:T(8,128)(2,1)S(1)} fusion(f32[16,8192]{1,0:T(8,128)S(1)} %get-tuple-element.504, f32[512]{0:T(512)S(1)} %multiply_reduce_fusion.9, f32[8192]{0:T(1024)S(1)} %get-tuple-element.502, f32[1,16,512]{2,0,1:T(1,128)S(1)} %constant_dynamic-slice_fusion.8), kind=kOutput, calls=%fused_computation.32.clone.1 | convolution fusion | flops 843055104 | bytes 8980480 | tf_op jit(solution)/shard_map/while/body/eval_jaxpr/dot_general | solution.py:11
  782.1 3.2 fusion.64
  785.4 23.0 %multiply_convert_fusion.8 = bf16[8192,512]{0,1:T(8,128)(2,1)S(1)} fusion(f32[16,8192]{1,0:T(8,128)S(1)} %get-tuple-element.504, f32[512]{0:T(512)S(1)} %multiply_reduce_fusion.9, f32[8192]{0:T(1024)S(1)} %get-tuple-element.502, f32[1,16,512]{2,0,1:T(1,128)S(1)} %constant_dynamic-slice_fusion.8), kind=kOutput, calls=%fused_computation.32.clone.1 | convolution fusion | flops 843055104 | bytes 8980480 | tf_op jit(solution)/shard_map/while/body/eval_jaxpr/dot_general | solution.py:11
  808.5 3.2 fusion.64
  811.8 23.0 %multiply_convert_fusion.8 = bf16[8192,512]{0,1:T(8,128)(2,1)S(1)} fusion(f32[16,8192]{1,0:T(8,128)S(1)} %get-tuple-element.504, f32[512]{0:T(512)S(1)} %multiply_reduce_fusion.9, f32[8192]{0:T(1024)S(1)} %get-tuple-element.502, f32[1,16,512]{2,0,1:T(1,128)S(1)} %constant_dynamic-slice_fusion.8), kind=kOutput, calls=%fused_computation.32.clone.1 | convolution fusion | flops 843055104 | bytes 8980480 | tf_op jit(solution)/shard_map/while/body/eval_jaxpr/dot_general | solution.py:11
  838.1 23.0 %multiply_convert_fusion.8 = bf16[8192,512]{0,1:T(8,128)(2,1)S(1)} fusion(f32[16,8192]{1,0:T(8,128)S(1)} %get-tuple-element.504, f32[512]{0:T(512)S(1)} %multiply_reduce_fusion.9, f32[8192]{0:T(1024)S(1)} %get-tuple-element.502, f32[1,16,512]{2,0,1:T(1,128)S(1)} %constant_dynamic-slice_fusion.8), kind=kOutput, calls=%fused_computation.32.clone.1 | convolution fusion | flops 843055104 | bytes 8980480 | tf_op jit(solution)/shard_map/while/body/eval_jaxpr/dot_general | solution.py:11
  864.4 23.0 %multiply_convert_fusion.8 = bf16[8192,512]{0,1:T(8,128)(2,1)S(1)} fusion(f32[16,8192]{1,0:T(8,128)S(1)} %get-tuple-element.504, f32[512]{0:T(512)S(1)} %multiply_reduce_fusion.9, f32[8192]{0:T(1024)S(1)} %get-tuple-element.502, f32[1,16,512]{2,0,1:T(1,128)S(1)} %constant_dynamic-slice_fusion.8), kind=kOutput, calls=%fused_computation.32.clone.1 | convolution fusion | flops 843055104 | bytes 8980480 | tf_op jit(solution)/shard_map/while/body/eval_jaxpr/dot_general | solution.py:11
  892.7 20.9 %reduce-scatter.2.cloned.1.call-done = f32[32,1024]{1,0:T(8,128)} async-done(((f32[32,4096]{1,0:T(8,128)}), f32[32,1024]{1,0:T(8,128)}) %reduce-scatter.2.cloned.1.call-update) | async-done | bytes 131088 | tf_op jit(solution)/shard_map/reduce_scatter | solution.py:67
  913.6 3.6 copy.78
  917.2 3.6 copy.79
  920.8 97.2 %all-reduce.8.cloned.1.call-done = f32[32,1024]{1,0:T(8,128)} async-done(((f32[32,1024]{1,0:T(8,128)}), f32[32,1024]{1,0:T(8,128)}) %all-reduce.8.cloned.1.call-update) | async-done | bytes 131088 | tf_op jit(solution)/shard_map/psum | solution.py:68
  (98 shorter events, 50.2 us)
Async XLA Ops:
  7.2 23.3 %copy-start = (f32[32,8192]{1,0:T(8,128)S(1)}, f32[32,8192]{1,0:T(8,128)}, u32[]{:S(2)}) copy-start(f32[32,8192]{1,0:T(8,128)} %param.17) | copy-start | bytes 3145732
  7.2 98.6 %all-gather.5.cloned.1.call-start = ((), (), s32[]{:S(2)}) async-start(), calls=%async_computation.5 | async-start | bytes 16908288 | tf_op jit(solution)/shard_map/all_gather | solution.py:53
  8.1 25.2 %copy-start.3 = (f32[1,2048]{1,0:T(1,128)}, f32[1,2048]{1,0:T(1,128)S(1)}, u32[]{:S(2)}) copy-start(f32[1,2048]{1,0:T(1,128)S(1)} %get-tuple-element.329) | copy-start | bytes 24580
  21.7 221.6 %all-gather.7.cloned.1.call-start = ((), (), s32[]{:S(2)}) async-start(), calls=%async_computation.6 | async-start | bytes 16908288 | tf_op jit(solution)/shard_map/all_gather | solution.py:53
  29.7 24.7 %copy-start.6 = (pred[2048]{0:T(1024)(128)(4,1)}, pred[2048]{0:T(1024)(128)(4,1)S(1)}, u32[]{:S(2)}) copy-start(pred[2048]{0:T(1024)(128)(4,1)S(1)} %compare_and_fusion) | copy-start | bytes 6148
  30.4 24.0 %copy-start.1 = (f32[16,8192]{1,0:T(8,128)S(1)}, f32[16,8192]{1,0:T(8,128)}, u32[]{:S(2)}) copy-start(f32[16,8192]{1,0:T(8,128)} %param.16) | copy-start | bytes 1572868
  30.4 334.5 %all-reduce.4.cloned.1.call-start = ((), (), s32[]{:S(2)}) async-start(), calls=%async_computation.1 | async-start | bytes 2097152 | tf_op jit(solution)/shard_map/psum | solution.py:59
  218.3 434.8 %all-reduce.6.cloned.1.call-start = ((), (), s32[]{:S(2)}) async-start(), calls=%async_computation.2 | async-start | bytes 2097152 | tf_op jit(solution)/shard_map/psum | solution.py:59
  389.0 113.1 %copy-start.2 = (f32[2048,32]{1,0:T(8,128)S(1)}, f32[2048,32]{1,0:T(8,128)}, u32[]{:S(2)}) copy-start(f32[2048,32]{1,0:T(8,128)} %gather_fusion.5) | copy-start | bytes 786436
  389.0 113.1 %copy-start.4 = (f32[1,2048]{1,0:T(1,128)S(1)}, f32[1,2048]{1,0:T(1,128)}, u32[]{:S(2)}) copy-start(f32[1,2048]{1,0:T(1,128)} %copy-done.3) | copy-start | bytes 24580
  389.0 113.1 %copy-start.7 = (pred[2048]{0:T(1024)(128)(4,1)S(1)}, pred[2048]{0:T(1024)(128)(4,1)}, u32[]{:S(2)}) copy-start(pred[2048]{0:T(1024)(128)(4,1)} %copy-done.6) | copy-start | bytes 6148
  491.9 12.9 %copy-start.5 = (f32[16,1024]{1,0:T(8,128)S(1)}, f32[16,1024]{1,0:T(8,128)}, u32[]{:S(2)}) copy-start(f32[16,1024]{1,0:T(8,128)} %param.21) | copy-start | bytes 196612
  504.7 408.9 %reduce-scatter.2.cloned.1.call-start = ((), (), s32[]{:S(2)}) async-start(), calls=%async_computation.3 | async-start | bytes 655360 | tf_op jit(solution)/shard_map/reduce_scatter | solution.py:67
  892.6 125.4 %all-reduce.8.cloned.1.call-start = ((), (), s32[]{:S(2)}) async-start(), calls=%async_computation.4 | async-start | bytes 262144 | tf_op jit(solution)/shard_map/psum | solution.py:68
Sparse Core Ops, SparseCore 0:
  21.8 83.9 all-gather.4
  109.0 79.8 all-gather.6
  218.5 146.4 all-reduce.3
  504.8 148.3 all-reduce.5
  892.8 20.7 reduce-scatter.1
  916.7 101.3 all-reduce.7
